TPU v7x, 256 devices: a whole 4x4x8 slice. The times are simulated.
256 devices in a mesh: prow: 8 (over x, core), pcol: 32 (over z, y).
Axes of the slice: x: 4, y: 4, z: 8, core: 2. Of those that a mesh axis runs over, the one named last changes fastest.
Arguments:
- anc_mask: int32 [2, 128], P(None, 'prow'), may hold values 0 or 1
- factor: bfloat16 [2, 16384, 2048], P(None, 'prow', 'pcol'), may hold values from -0.046875 to 0.046875
- inverse_block: bfloat16 [16384, 16384], P('prow', 'pcol'), may hold values from -6 to 6
- diag_inverse: float32 [2, 2048, 2048], P(None, 'prow', 'pcol'), may hold values from -6 to 6
Outputs:
- offdiag: float32 [2, 2048, 16384], P(None, 'prow', 'pcol')
- diag_block: float32 [2, 2048, 2048], P(None, 'prow', 'pcol')
All inputs are finite; a program needn't handle non-finite values. No bound on the sum of `anc_mask` on one device may be relied on, other than what follows from the above.
Results may differ from a plain program's by a relative error of at most 0.0017.
Values may be sent and summed in bfloat16 or wider, within the bound.
A program may use at most 128 MiB of HBM per device.

v0:
```python
import jax
import jax.numpy as jnp
from jax import lax
from jax.sharding import PartitionSpec as P


def spread(value, axis, source):
    kept = jnp.where(lax.axis_index(axis) == source, value, 0).astype(value.dtype)
    return lax.psum(kept, axis)


def finish(count, summed, cols_q, lq_rows):
    wide_p = summed.shape[0]
    off_local = (-summed).reshape(wide_p, count, cols_q).transpose(1, 0, 2)
    off_round = off_local.astype(jnp.bfloat16)
    partial_diag = jnp.einsum(
        "swr,srv->swv", off_round, lq_rows, preferred_element_type=jnp.float32
    )
    return (off_local, partial_diag)


def cross_place(cols_q):
    ratio = lax.axis_size("pcol") // lax.axis_size("prow")
    column = lax.axis_index("pcol")
    offset = column % ratio * cols_q
    return (offset, column // ratio)


def shards(anc_mask, factor, inverse_block, diag_inverse):
    block_rows = factor.shape[1] // anc_mask.shape[1]
    row_mask = jnp.repeat(anc_mask, block_rows, axis=1).astype(jnp.bfloat16)
    masked = factor * row_mask[:, :, None]
    count = masked.shape[0]
    cols_q = inverse_block.shape[1]
    offset, root = cross_place(cols_q)
    gathered = lax.all_gather(masked, "pcol", axis=2, tiled=True)
    wide = gathered.shape[2]
    term = jnp.einsum("src,rq->csq", gathered, inverse_block, preferred_element_type=jnp.float32)
    summed = lax.psum_scatter(
        term.reshape(wide // lax.axis_size("prow") * lax.axis_size("prow"), count * cols_q),
        "prow",
        scatter_dimension=0,
        tiled=True,
    )
    piece_rows = lax.dynamic_slice_in_dim(gathered, offset, cols_q, 1)
    lq_rows = spread(piece_rows, "prow", root)
    off_local, partial_diag = finish(count, summed, cols_q, lq_rows)
    reduced = lax.psum_scatter(partial_diag, "pcol", scatter_dimension=2, tiled=True)
    return (off_local, diag_inverse - reduced)


def solution(mesh):
    placed = (P(None, "prow"), P(None, "prow", "pcol"), P("prow", "pcol"), P(None, "prow", "pcol"))
    return jax.shard_map(
        shards,
        mesh=mesh,
        in_specs=placed,
        out_specs=(P(None, "prow", "pcol"), P(None, "prow", "pcol")),
        check_vma=False,
    )
```

profile of v0, /device:TPU:6, one launch (start us, length us, event | category | flops | bytes accessed | tf_op | source)
XLA Modules:
  0.0 536.3 jit_solution(1170632317607449132)
XLA Ops:
  7.2 0.0 copy-start
  7.2 0.0 all-gather.2.cloned.1.call-start
  7.2 0.8 convert_element_type.16
  8.0 0.1 broadcast_bitcast_fusion
  8.1 1.9 broadcast_multiply_fusion
  10.0 0.0 all-gather.2.cloned.1.call-update
  10.0 0.0 reduce-scatter.3.cloned.1.call-start
  10.1 144.6 %all-gather.2.cloned.1.call-done = bf16[2,2048,2048]{1,2,0:T(8,128)(2,1)} async-done(((bf16[2,2048,64]{1,2,0:T(8,128)(2,1)}), bf16[2,2048,2048]{1,2,0:T(8,128)(2,1)}) %all-gather.2.cloned.1.call-update) | async-done | bytes 16777232 | tf_op jit(solution)/shard_map/all_gather | solution.py:36
  154.7 0.0 copy-done
  154.7 14.5 %fusion = f32[2,2048,512]{1,2,0:T(8,128)} fusion(bf16[2,2048,2048]{1,2,0:T(8,128)(2,1)} %all-gather.2.cloned.1.call-done, bf16[2048,512]{1,0:T(8,128)(2,1)S(1)} %copy-done), kind=kOutput, calls=%fused_computation.1 | convolution fusion | flops 8589934592 | bytes 27262976 | tf_op jit(solution)/shard_map/src,rq->csq/dot_general | solution.py:38
  169.2 0.0 reduce-scatter.3.cloned.1.call-update
  169.2 0.0 all-reduce.2.cloned.1.call-start
  169.3 4.9 dynamic-slice_select_fusion
  174.2 0.0 all-reduce.2.cloned.1.call-update
  174.2 0.0 reduce-scatter.5.cloned.1.call-start
  174.3 45.3 %reduce-scatter.3.cloned.1.call-done = f32[256,1024]{0,1:T(8,128)} async-done(((f32[2048,1024]{0,1:T(8,128)}), f32[256,1024]{0,1:T(8,128)}) %reduce-scatter.3.cloned.1.call-update) | async-done | bytes 1048592 | tf_op jit(solution)/shard_map/reduce_scatter | solution.py:39
  219.6 1.3 neg.3
  220.9 77.6 %all-reduce.2.cloned.1.call-done = bf16[2,512,2048]{1,2,0:T(8,128)(2,1)} async-done(((bf16[2,512,2048]{1,2,0:T(8,128)(2,1)}), bf16[2,512,2048]{1,2,0:T(8,128)(2,1)}) %all-reduce.2.cloned.1.call-update) | async-done | bytes 4194320 | tf_op jit(solution)/shard_map/psum | solution.py:9
  298.5 5.4 %fusion.2 = f32[2,256,2048]{1,2,0:T(8,128)} fusion(bf16[2,512,2048]{1,2,0:T(8,128)(2,1)} %all-reduce.2.cloned.1.call-done, f32[2,256,512]{1,2,0:T(8,128)S(1)} %bitcast.16), kind=kOutput, calls=%fused_computation.3 | convolution fusion | flops 1074003968 | bytes 9437184 | tf_op jit(solution)/shard_map/swr,srv->swv/dot_general | solution.py:16
  303.9 0.0 reduce-scatter.5.cloned.1.call-update
  304.0 1.3 copy.9
  305.3 222.9 %reduce-scatter.5.cloned.1.call-done = f32[2,256,64]{1,2,0:T(8,128)} async-done(((f32[2,256,2048]{1,2,0:T(8,128)}), f32[2,256,64]{1,2,0:T(8,128)}) %reduce-scatter.5.cloned.1.call-update) | async-done | bytes 131088 | tf_op jit(solution)/shard_map/reduce_scatter | solution.py:48
  528.2 0.0 copy-done.1
  528.2 1.6 sub.8
  (2 shorter events, 0.0 us)
Async XLA Ops:
  7.2 147.5 %copy-start = (bf16[2048,512]{1,0:T(8,128)(2,1)S(1)}, bf16[2048,512]{1,0:T(8,128)(2,1)}, u32[]{:S(2)}) copy-start(bf16[2048,512]{1,0:T(8,128)(2,1)} %param.6) | copy-start | bytes 6291460
  7.2 147.5 %all-gather.2.cloned.1.call-start = ((), (), s32[]{:S(2)}) async-start(), calls=%async_computation.2 | async-start | bytes 17301504 | tf_op jit(solution)/shard_map/all_gather | solution.py:36
  10.0 209.5 %reduce-scatter.3.cloned.1.call-start = ((), (), s32[]{:S(2)}) async-start(), calls=%async_computation.3 | async-start | bytes 9437184 | tf_op jit(solution)/shard_map/reduce_scatter | solution.py:39
  169.2 129.3 %all-reduce.2.cloned.1.call-start = ((), (), s32[]{:S(2)}) async-start(), calls=%async_computation.4 | async-start | bytes 8388608 | tf_op jit(solution)/shard_map/psum | solution.py:9
  174.2 354.0 %reduce-scatter.5.cloned.1.call-start = ((), (), s32[]{:S(2)}) async-start(), calls=%async_computation.5 | async-start | bytes 4325376 | tf_op jit(solution)/shard_map/reduce_scatter | solution.py:48
  303.9 224.2 %copy-start.1 = (f32[2,256,64]{1,2,0:T(8,128)S(1)}, f32[2,256,64]{1,2,0:T(8,128)}, u32[]{:S(2)}) copy-start(f32[2,256,64]{1,2,0:T(8,128)} %param.7) | copy-start | bytes 393220
Sparse Core Ops, SparseCore 0:
  11.2 143.4 all-gather.1
  169.4 50.1 reduce-scatter.2
  221.9 76.5 all-reduce.1
  304.1 224.0 reduce-scatter.4
where the time goes:
time: 537 us; the launch traced here: 536 us
  waiting for transfers between devices  491 us (91%)
  matrix products  20 us (4%)
  between operations  13.8 us (3%)
  other arithmetic  10.5 us (2%)
    reduce_scatter x1, waiting for transfers between devices, shards(): lax.psum_scatter(partial_diag, 'pcol', scatter_dimension=2, tiled=True)  223 us
    all_gather x1, waiting for transfers between devices, shards(): gathered = lax.all_gather(masked, 'pcol', axis=2, tiled=True)  145 us
    psum x1, waiting for transfers between devices, spread(): return lax.psum(kept, axis)  77.6 us
    reduce_scatter x1, waiting for transfers between devices, shards(): lax.psum_scatter(term.reshape(wide // lax.axis_size('prow') * lax.axis_si...  45.3 us
    dot_general x1, matrix products, shards(): jnp.einsum('src,rq->csq', gathered, inverse_block, preferred_element_type...  14.5 us
  transfers between devices with their start and end apart: 4, of which 4 were waited for; matrix products, arithmetic and copies ran while one was open for 1% of the time, Pallas kernels for 0%

commit v1 on v0

v1 whole, which is shorter than its diff:
```python
import jax
import jax.numpy as jnp
from jax import lax
from jax.experimental import pallas as pl
from jax.experimental.pallas import tpu as pltpu
from jax.sharding import PartitionSpec as P

MESH = pl.DeviceIdType.MESH
F32 = jnp.float32
BF16 = jnp.bfloat16


def mod(value, size):
    return lax.rem(value + size, size)


def remote(src, dst, send, recv, device):
    return pltpu.make_async_remote_copy(
        src_ref=src, dst_ref=dst, send_sem=send, recv_sem=recv, device_id=device, device_id_type=MESH
    )


def kernel(
    mask_ref, f_ref, b_ref, dinv_ref, off_ref, diag_ref,
    mf, b1, b2, stage, ks, rbuf, xbuf, m2, oq, pt, zbuf, dfin,
    mzs, mzr, mys, myr, pts, ptr, css, csr, xss, xsr, m2xs, m2xr, m2cs, m2cr, m2l, oqs, oqr, zss, zsr, loc,
):
    i = lax.axis_index("prow")
    j = lax.axis_index("pcol")
    x, c = lax.div(i, 2), lax.rem(i, 2)
    z, y = lax.div(j, 4), lax.rem(j, 4)
    a = lax.div(y, 2)
    y1 = y + 1 - 2 * lax.rem(y, 2)
    yp = 3 - y
    y1p = 3 - y1
    slots = (y, y1, yp)

    def dev(x_, c_, z_, y_):
        return (2 * x_ + c_, 4 * z_ + y_)

    mate = dev(x, c, z, yp)
    beside = dev(x, c, z, y1)
    zdev = (dev(x, c, mod(z + 1, 8), y), dev(x, c, mod(z - 1, 8), y))
    sib = dev(x, 1 - c, z, y)

    own_b = pltpu.make_async_copy(b_ref, b1, loc.at[0])
    own_b.start()

    def slot(zb, s, low=0, rows=64):
        return mf.at[zb, pl.ds(pl.multiple_of(64 * s + low, 32), rows)]

    @pl.loop(0, 16)
    def _(b):
        lanes = pl.ds(pl.multiple_of(128 * b, 128), 128)
        keep = mask_ref[a, b].astype(F32)
        mf[z, pl.ds(pl.multiple_of(64 * y, 64), 64), lanes] = (f_ref[a, :, lanes].astype(F32) * keep).astype(BF16)
        other = mask_ref[1 - a, b].astype(F32)
        stage[:, lanes] = (f_ref[1 - a, :, lanes].astype(F32) * other).astype(BF16)

    barrier = pltpu.get_barrier_semaphore()
    greeted = [mate, beside, zdev[0], zdev[1], sib] + [dev(mod(x + k, 4), c, z, y) for k in (1, 2, 3)]
    for device in greeted:
        pl.semaphore_signal(barrier, inc=1, device_id=device, device_id_type=MESH)
    pl.semaphore_wait(barrier, len(greeted))

    def ring(way, t, p, sent):
        sign = 1 if way else -1
        zb = mod(z + sign * (t - 1 if sent else t), 8)
        if t == 4 and p == 2:
            part = slot(zb, slots[2], 32 * way, 32)
        else:
            part = slot(zb, slots[p])
        return remote(part, part, mzs.at[way, t, p], mzr.at[way, t, p], zdev[way])

    ring_steps = [(way, t, p) for t in (1, 2, 3) for p in range(3) for way in (0, 1)]
    ring_steps += [(0, 4, 0), (1, 4, 1), (0, 4, 2), (1, 4, 2)]

    mate_m = remote(stage, slot(z, y), pts.at[0], ptr.at[0], mate)
    mate_b = remote(b_ref, b2, pts.at[1], ptr.at[1], mate)
    beside_a = remote(slot(z, y), slot(z, y), mys.at[8], myr.at[8], beside)

    def beside_b(zb, sent):
        part = slot(zb, yp if sent else y1p)
        return remote(part, part, mys.at[zb], myr.at[zb], beside)

    e = mod(x - lax.div(z, 2), 4)
    col = c == lax.rem(z, 2)
    source = jnp.logical_and(col, e == 0)
    relay = jnp.logical_and(col, e > 0)

    def m2_part(zb, kind):
        return m2.at[zb, pl.ds(pl.multiple_of(64 * kind, 64), 64)]

    def m2_along(zb, kind, first):
        device = dev(mod(x + 1 + 2 * kind, 4), c, z, y)
        src = slot(zb, y + kind * (3 - 2 * y)) if first else m2_part(zb, kind)
        return remote(src, m2_part(zb, kind), m2xs.at[kind, zb], m2xr.at[kind, zb], device)

    def m2_across(zb, kind, first):
        src = slot(zb, y + kind * (3 - 2 * y)) if first else m2_part(zb, kind)
        return remote(src, m2_part(zb, kind), m2cs.at[kind, zb], m2cr.at[kind, zb], sib)

    def m2_here(zb, kind):
        return pltpu.make_async_copy(slot(zb, y + kind * (3 - 2 * y)), m2_part(zb, kind), m2l.at[kind, zb])

    def hops(kind):
        return e + kind * (4 - 2 * e)

    def m2_stage(tau):
        @pl.loop(0, 4)
        def _(q):
            kind, way = lax.div(q, 2), lax.rem(q, 2)
            if tau <= 4:
                fits = jnp.logical_and(tau >= way, tau <= 4 - way)

                @pl.when(jnp.logical_and(source, fits))
                def _():
                    zb = mod(z + (2 * way - 1) * tau, 8)
                    m2_along(zb, kind, True).start()
                    m2_across(zb, kind, True).start()
                    m2_here(zb, kind).start()

            t = tau - hops(kind)
            due = jnp.logical_and(t >= way, t <= 4 - way)

            @pl.when(jnp.logical_and(relay, due))
            def _():
                zb = mod(z + (2 * way - 1) * t, 8)
                m2_along(zb, kind, False).wait_recv()

                @pl.when(hops(kind) < 3)
                def _():
                    m2_along(zb, kind, False).start()

                m2_across(zb, kind, False).start()

    def core_copy(zb, h):
        return remote(ks.at[zb, h], rbuf.at[h, lax.div(zb, 2)], css.at[h, zb], csr.at[h, zb], sib)

    def x_copy(zb, h):
        owner = lax.div(zb, 2)
        place = mod(x - owner, 4) - 1
        return remote(ks.at[zb, h], xbuf.at[place, h], xss.at[h, zb], xsr.at[h, place], dev(owner, c, z, y))

    def unit(zb, h):
        right = (b1, b2)[h]

        @pl.loop(0, 2)
        def _(n):
            lanes = pl.ds(pl.multiple_of(256 * n, 256), 256)
            ks[zb, h, :, lanes] = jnp.dot(mf[zb], right[:, lanes], preferred_element_type=F32)

        @pl.when(lax.rem(zb, 2) != c)
        def _():
            core_copy(zb, h).start()

    def merge(zb, h):
        @pl.when(lax.rem(zb, 2) == c)
        def _():
            core_copy(zb, h).wait_recv()
            ks[zb, h] = ks[zb, h] + rbuf[h, lax.div(zb, 2)]

            @pl.when(lax.div(zb, 2) != x)
            def _():
                x_copy(zb, h).start()

    mate_m.start()
    beside_a.start()
    ring(0, 1, 0, True).start()
    ring(1, 1, 0, True).start()
    mate_b.start()
    beside_a.wait_recv()
    ring(0, 1, 1, True).start()
    ring(1, 1, 1, True).start()
    mate_m.wait_recv()
    ring(0, 1, 2, True).start()
    ring(1, 1, 2, True).start()
    beside_b(z, True).start()
    m2_stage(0)
    own_b.wait()
    beside_b(z, False).wait_recv()
    unit(z, 0)
    merge(z, 0)

    for t in (1, 2, 3):
        near = (mod(z - t, 8), mod(z + t, 8))
        for p in range(3):
            for way in (0, 1):
                ring(way, t, p, False).wait_recv()
                if (way, t + 1, p) in ring_steps:
                    ring(way, t + 1, p, True).start()
                if p == 2:
                    beside_b(near[way], True).start()
        m2_stage(t)
        for zb in near:
            beside_b(zb, False).wait_recv()
            unit(zb, 0)
        for zb in near:
            merge(zb, 0)

    mate_b.wait_recv()

    @pl.loop(0, 7)
    def _(n):
        unit(mod(z + n - 3, 8), 1)

        @pl.when(n > 0)
        def _():
            merge(mod(z + n - 4, 8), 1)

    merge(mod(z + 3, 8), 1)

    far = mod(z + 4, 8)
    for way, t, p in ring_steps[-4:]:
        ring(way, t, p, False).wait_recv()
    beside_b(far, True).start()
    m2_stage(4)
    beside_b(far, False).wait_recv()
    unit(far, 0)
    unit(far, 1)
    merge(far, 0)
    merge(far, 1)
    m2_stage(5)

    def oq_part(s):
        return oq.at[:, pl.ds(pl.multiple_of(512 * s, 512), 512)]

    def oq_copy(h, sent):
        s = ((y, yp) if sent else (y1, y1p))[h]
        return remote(oq_part(s), oq_part(s), oqs.at[h], oqr.at[h], beside)

    off_here = pltpu.make_async_copy(ks.at[i, 0], off_ref.at[a], loc.at[1])
    off_there = remote(ks.at[i, 1], off_ref.at[a], pts.at[2], ptr.at[2], mate)
    for h in (0, 1):
        for place in range(3):
            remote(ks.at[i, h], xbuf.at[place, h], xss.at[h, i], xsr.at[h, place], sib).wait_recv()
        ks[i, h] = -((ks[i, h] + xbuf[0, h]) + (xbuf[1, h] + xbuf[2, h]))
        oq[:, pl.ds(pl.multiple_of(512 * (y, yp)[h], 512), 512)] = ks[i, h].astype(BF16)
        oq_copy(h, True).start()
        (off_here, off_there)[h].start()
    m2_stage(6)
    m2_stage(7)

    @pl.loop(0, 16)
    def _(q):
        zb, kind = lax.div(q, 2), lax.rem(q, 2)

        @pl.when(source)
        def _():
            m2_here(zb, kind).wait()

        @pl.when(jnp.logical_not(col))
        def _():
            m2_across(zb, kind, False).wait_recv()

    for h in (0, 1):
        oq_copy(h, False).wait_recv()

    @pl.loop(0, 8)
    def _(zb):
        pt[zb] = lax.dot_general(m2[zb], oq[...], (((1,), (1,)), ((), ())), preferred_element_type=F32)

    def z_copy(way, k, kind):
        sign = -1 if way else 1
        zb = mod(z + sign * (5 - k), 8)
        return remote(
            pt.at[zb, pl.ds(64 * kind, 64)], zbuf.at[way, k - 1, kind], zss.at[way, k, kind], zsr.at[way, k, kind], zdev[way]
        )

    def z_has(way, k, kind):
        return k > 1 or kind == way

    for k in (1, 2, 3, 4, 5):
        for kind in (0, 1):
            for way in (0, 1):
                if k > 1 and z_has(way, k - 1, kind):
                    z_copy(way, k - 1, kind).wait_recv()
                    zb = mod(z + (-1 if way else 1) * (5 - k), 8)
                    rows = pl.ds(64 * kind, 64)
                    pt[zb, rows] = pt[zb, rows] + zbuf[way, k - 2, kind]
                if k < 5 and z_has(way, k, kind):
                    z_copy(way, k, kind).start()

    last = remote(pt.at[z, pl.ds(64, 64)], dfin, pts.at[3], ptr.at[3], mate)
    last.start()
    diag_ref[a] = dinv_ref[a] - pt[z, pl.ds(0, 64)]
    last.wait_recv()
    diag_ref[1 - a] = dinv_ref[1 - a] - dfin[...]

    last.wait_send()
    off_here.wait()
    off_there.wait_send()
    off_there.wait_recv()
    mate_m.wait_send()
    mate_b.wait_send()
    beside_a.wait_send()
    for way, t, p in ring_steps:
        ring(way, t, p, True).wait_send()
    for h in (0, 1):
        oq_copy(h, True).wait_send()
    for k in (1, 2, 3, 4):
        for kind in (0, 1):
            for way in (0, 1):
                if z_has(way, k, kind):
                    z_copy(way, k, kind).wait_send()

    @pl.loop(0, 8)
    def _(zb):
        beside_b(zb, True).wait_send()
        for h in (0, 1):
            @pl.when(lax.rem(zb, 2) != c)
            def _():
                core_copy(zb, h).wait_send()

            @pl.when(jnp.logical_and(lax.rem(zb, 2) == c, lax.div(zb, 2) != x))
            def _():
                x_copy(zb, h).wait_send()

        for kind in (0, 1):
            @pl.when(col)
            def _():
                m2_across(zb, kind, False).wait_send()

                @pl.when(jnp.logical_or(e == 0, hops(kind) < 3))
                def _():
                    m2_along(zb, kind, False).wait_send()


def shards(anc_mask, factor, inverse_block, diag_inverse):
    vmem = pl.BlockSpec(memory_space=pltpu.VMEM)
    hbm = pl.BlockSpec(memory_space=pl.ANY)
    dma = pltpu.SemaphoreType.DMA
    off, diag = pl.pallas_call(
        kernel,
        out_shape=(jax.ShapeDtypeStruct((2, 256, 512), F32), jax.ShapeDtypeStruct((2, 64, 256), F32)),
        in_specs=[pl.BlockSpec(memory_space=pltpu.SMEM), vmem, hbm, vmem],
        out_specs=(hbm, vmem),
        scratch_shapes=[
            pltpu.VMEM((8, 256, 2048), BF16),
            pltpu.VMEM((2048, 512), BF16),
            pltpu.VMEM((2048, 512), BF16),
            pltpu.VMEM((64, 2048), BF16),
            pltpu.VMEM((8, 2, 256, 512), F32),
            pltpu.VMEM((2, 4, 256, 512), F32),
            pltpu.VMEM((3, 2, 256, 512), F32),
            pltpu.VMEM((8, 128, 2048), BF16),
            pltpu.VMEM((256, 2048), BF16),
            pltpu.VMEM((8, 128, 256), F32),
            pltpu.VMEM((2, 4, 2, 64, 256), F32),
            pltpu.VMEM((64, 256), F32),
            dma((2, 5, 3)), dma((2, 5, 3)),
            dma((9,)), dma((9,)),
            dma((4,)), dma((4,)),
            dma((2, 8)), dma((2, 8)),
            dma((2, 8)), dma((2, 3)),
            dma((2, 8)), dma((2, 8)), dma((2, 8)), dma((2, 8)), dma((2, 8)),
            dma((2,)), dma((2,)),
            dma((2, 5, 2)), dma((2, 5, 2)),
            dma((2,)),
        ],
        compiler_params=pltpu.CompilerParams(
            collective_id=0, has_side_effects=True, vmem_limit_bytes=52 * 2**20
        ),
        cost_estimate=pl.CostEstimate(flops=9663676416, bytes_accessed=2**23, transcendentals=0),
        name="selected_inverse",
    )(anc_mask, factor.transpose(0, 2, 1), inverse_block, diag_inverse.transpose(0, 2, 1))
    return off, diag.transpose(0, 2, 1)


def solution(mesh):
    placed = (P(None, "prow"), P(None, "prow", "pcol"), P("prow", "pcol"), P(None, "prow", "pcol"))
    return jax.shard_map(
        shards,
        mesh=mesh,
        in_specs=placed,
        out_specs=(P(None, "prow", "pcol"), P(None, "prow", "pcol")),
        check_vma=False,
    )
```

time: 537 us -> 167 us (0.31)
  waiting for transfers between devices: 491 us -> 0 us
  Pallas kernels: 0 us -> 162 us
  matrix products: 20 us -> 0 us
  between operations: 13.8 us -> 0.65 us
  other arithmetic: 10.5 us -> 0 us
    reduce_scatter x2 -> x0, waiting for transfers between devices: 268 us -> none  [the longest x1 223 us: shards(): lax.psum_scatter(partial_diag, 'pcol', scatter_dimension=2, tiled=True)]
    pallas_call x0 -> x1, Pallas kernels: none -> 162 us  [shards(): pl.pallas_call(kernel, out_shape=(jax.ShapeDtypeStruct((2, 256, 512), F32...]
    all_gather x1 -> x0, waiting for transfers between devices: 145 us -> none  [shards(): gathered = lax.all_gather(masked, 'pcol', axis=2, tiled=True)]
    psum x1 -> x0, waiting for transfers between devices: 77.6 us -> none  [spread(): return lax.psum(kept, axis)]
    dot_general x2 -> x0, matrix products: 20 us -> none  [the longest x1 14.5 us: shards(): jnp.einsum('src,rq->csq', gathered, inverse_block, preferred_element_type...]
  transfers between devices with their start and end apart: 4 -> 0, of which waited for: 4 -> 0; matrix products, arithmetic and copies ran while one was open for 1% -> 0% of each run, Pallas kernels for 0% -> 0%
where the time goes in v1:
time: 167 us
  Pallas kernels  162 us (97%)
  local copies, waits for them, and re-layouts  4.24 us (3%)
    pallas_call x1, Pallas kernels, shards(): pl.pallas_call(kernel, out_shape=(jax.ShapeDtypeStruct((2, 256, 512), F32...  162 us
    unnamed x8, local copies, waits for them, and re-layouts  4.24 us

profile of v1, /device:TPU:6, one launch (start us, length us, event | category | flops | bytes accessed | tf_op | source)
XLA Modules:
  0.0 167.2 jit_solution(14682483651189534480)
XLA Ops:
  0.6 0.0 copy-start
  0.6 1.0 copy-done
  1.7 0.0 copy-start.1
  1.7 0.9 copy-done.1
  2.6 0.0 copy-start.2
  2.6 0.7 copy-done.2
  3.3 162.3 %selected_inverse.1 = (f32[2,256,512]{2,1,0:T(8,128)S(1)}, f32[2,64,256]{2,1,0:T(8,128)S(1)}) custom-call(s32[2,16]{1,0:T(2,128)S(1)} %copy-done.2, bf16[2,64,2048]{2,1,0:T(8,128)(2,1)S(1)} %bitcast.4, bf16[2048,512]{1,0:T(8,128)(2,1)} %b_ref.1, f32[2,64,256]{2,1,0:T(8,128)S(1)} %bitcast.5), custom_call_target="tpu_custom_call" | custom-call | flops 9663676416 | bytes 8388608 | tf_op jit(solution)/shard_map/selected_inverse/pallas_call | solution.py:333
  165.6 1.0 copy.8
  166.6 0.7 copy.9
Async XLA Ops:
  0.6 1.0 copy-start
  1.7 0.9 copy-start.1
  2.6 0.7 copy-start.2

commit v2 on v0

v2 whole, which is shorter than its diff:
```python
import jax
import jax.numpy as jnp
from jax import lax
from jax.experimental import pallas as pl
from jax.experimental.pallas import tpu as pltpu
from jax.sharding import PartitionSpec as P

MESH = pl.DeviceIdType.MESH
F32 = jnp.float32
BF16 = jnp.bfloat16
H = 2
SR = 64 // H
WR = 256 // H


def mod(value, size):
    return lax.rem(value + size, size)


def remote(src, dst, send, recv, device):
    return pltpu.make_async_remote_copy(
        src_ref=src, dst_ref=dst, send_sem=send, recv_sem=recv, device_id=device, device_id_type=MESH
    )


def kernel(
    mask_hbm, f_hbm, b_ref, dinv_hbm, off_ref, diag_ref,
    mask_ref, f_ref, dinv_ref, mf, b1, b2, stage, ks, rbuf, xbuf, hbuf, m2, oq, pt, zbuf, dfin,
    mzs, mzr, mas, mar, mys, myr, mms, mmr, pts, ptr, css, csr, xss, xsr, hsr,
    m2xs, m2xr, m2cs, m2cr, m2l, oqs, oqr, offs, offr, zss, zsr, dfs, dfr, loc,
):
    i = lax.axis_index("prow")
    j = lax.axis_index("pcol")
    x, c = lax.div(i, 2), lax.rem(i, 2)
    z, y = lax.div(j, 4), lax.rem(j, 4)
    a = lax.div(y, 2)
    y1 = y + 1 - 2 * lax.rem(y, 2)
    yp = 3 - y
    y1p = 3 - y1
    slots = (y, y1, yp)

    def dev(x_, c_, z_, y_):
        return (2 * x_ + c_, 4 * z_ + y_)

    mate = dev(x, c, z, yp)
    beside = dev(x, c, z, y1)
    zdev = (dev(x, c, mod(z + 1, 8), y), dev(x, c, mod(z - 1, 8), y))
    xdev = (dev(mod(x + 1, 4), c, z, y), dev(mod(x - 1, 4), c, z, y))
    sib = dev(x, 1 - c, z, y)

    loads = [
        pltpu.make_async_copy(src, dst, loc.at[n])
        for n, (src, dst) in enumerate(((mask_hbm, mask_ref), (f_hbm, f_ref), (b_ref, b1), (dinv_hbm, dinv_ref)))
    ]
    for load in loads:
        load.start()
    barrier = pltpu.get_barrier_semaphore()
    greeted = [mate, beside, zdev[0], zdev[1], xdev[0], xdev[1], sib]
    for device in greeted:
        pl.semaphore_signal(barrier, inc=1, device_id=device, device_id_type=MESH)
    loads[0].wait()
    loads[1].wait()

    @pl.loop(0, 16)
    def _(b):
        lanes = pl.ds(pl.multiple_of(128 * b, 128), 128)
        keep = mask_ref[a, b].astype(F32)
        other = mask_ref[1 - a, b].astype(F32)
        for hf in range(H):
            rows = pl.ds(SR * hf, SR)
            mf[z, hf, y, :, lanes] = (f_ref[a, rows, lanes].astype(F32) * keep).astype(BF16)
            stage[hf, :, lanes] = (f_ref[1 - a, rows, lanes].astype(F32) * other).astype(BF16)

    pl.semaphore_wait(barrier, len(greeted))

    def ring(way, hf, t, p, sent):
        sign = 1 if way else -1
        zb = mod(z + sign * (t - 1 if sent else t), 8)
        part = mf.at[zb, hf, slots[p]]
        if t == 4 and p == 2:
            part = mf.at[zb, hf, slots[2], pl.ds(SR // 2 * way, SR // 2)]
        return remote(part, part, mzs.at[hf, way, t, p], mzr.at[hf, way, t, p], zdev[way])

    near_steps = [(way, t, p) for t in (1, 2, 3) for p in range(3) for way in (0, 1)]
    far_steps = [(0, 4, 0), (1, 4, 1), (0, 4, 2), (1, 4, 2)]
    ring_steps = near_steps + far_steps

    def mate_m(hf):
        return remote(stage.at[hf], mf.at[z, hf, y], mms.at[hf], mmr.at[hf], mate)

    def mate_b(n):
        lanes = pl.ds(256 * n, 256)
        return remote(b_ref.at[:, lanes], b2.at[:, lanes], pts.at[n], ptr.at[n], mate)

    def beside_a(hf):
        return remote(mf.at[z, hf, y], mf.at[z, hf, y], mas.at[hf], mar.at[hf], beside)

    def beside_b(zb, hf, sent):
        part = mf.at[zb, hf, yp if sent else y1p]
        return remote(part, part, mys.at[hf, zb], myr.at[hf, zb], beside)

    e = mod(x - lax.div(z, 2), 4)
    col = c == lax.rem(z, 2)
    source = jnp.logical_and(col, e == 0)
    relay = jnp.logical_and(col, e > 0)

    def m2_part(zb, hf, kind):
        return m2.at[zb, pl.ds(pl.multiple_of(64 * kind + SR * hf, SR), SR)]

    def m2_from(zb, hf, kind, first):
        return mf.at[zb, hf, y + kind * (3 - 2 * y)] if first else m2_part(zb, hf, kind)

    def m2_along(zb, hf, kind, first):
        device = dev(mod(x + 1 + 2 * kind, 4), c, z, y)
        return remote(
            m2_from(zb, hf, kind, first), m2_part(zb, hf, kind), m2xs.at[hf, kind, zb], m2xr.at[hf, kind, zb], device
        )

    def m2_across(zb, hf, kind, first):
        return remote(
            m2_from(zb, hf, kind, first), m2_part(zb, hf, kind), m2cs.at[hf, kind, zb], m2cr.at[hf, kind, zb], sib
        )

    def m2_here(zb, hf, kind):
        return pltpu.make_async_copy(m2_from(zb, hf, kind, True), m2_part(zb, hf, kind), m2l.at[hf, kind, zb])

    def hops(kind):
        return e + kind * (4 - 2 * e)

    def m2_stage(tau):
        @pl.loop(0, 4)
        def _(q):
            kind, way = lax.div(q, 2), lax.rem(q, 2)
            if tau < 5 * H:
                fits = jnp.logical_and(tau % 5 >= way, tau % 5 <= 4 - way)

                @pl.when(jnp.logical_and(source, fits))
                def _():
                    zb = mod(z + (2 * way - 1) * (tau % 5), 8)
                    m2_along(zb, tau // 5, kind, True).start()
                    m2_across(zb, tau // 5, kind, True).start()
                    m2_here(zb, tau // 5, kind).start()

            n = tau - hops(kind)
            t = lax.rem(n + 5, 5)
            due = jnp.logical_and(jnp.logical_and(n >= 0, n < 5 * H), jnp.logical_and(t >= way, t <= 4 - way))

            @pl.when(jnp.logical_and(relay, due))
            def _():
                hf = lax.div(n, 5)
                zb = mod(z + (2 * way - 1) * t, 8)
                m2_along(zb, hf, kind, False).wait_recv()

                @pl.when(hops(kind) < 3)
                def _():
                    m2_along(zb, hf, kind, False).start()

                m2_across(zb, hf, kind, False).start()

    def window(g):
        return (0, 0, 512) if g == 0 else (1, 256 * (g - 1), 256)

    def tile(ref, g, index, rows=pl.ds(0, 4)):
        h, low, width = window(g)
        return ref.at[index + (h, rows, pl.ds(0, SR), pl.ds(low, width))]

    def core_copy(zb, hf, g):
        return remote(
            tile(ks, g, (zb, hf)), tile(rbuf, g, (lax.div(zb, 2), hf)), css.at[hf, g, zb], csr.at[hf, g, zb], sib
        )

    def unit(zb, hf, g):
        h, low, width = window(g)
        left = mf[zb, hf].reshape(WR, 2048)
        right = (b1, b2)[h]
        for at in range(low, low + width, 256):
            lanes = pl.ds(at, 256)
            ks[zb, hf, h, :, :, lanes] = jnp.dot(left, right[:, lanes], preferred_element_type=F32).reshape(4, SR, 256)

        @pl.when(lax.rem(zb, 2) != c)
        def _():
            core_copy(zb, hf, g).start()

    def place(zb, hh):
        return mod((1 - 2 * hh) * (lax.div(zb, 2) - x), 4)

    def x_copy(zb, hf, g, hh, dst, recv, device):
        src = tile(ks, g, (zb, hf), pl.ds(2 * hh, 2))
        h, low, width = window(g)
        return remote(
            src, dst.at[:, :, pl.ds(low, width)], xss.at[hf, g, hh, zb], recv, device
        )

    def x_direct(zb, hf, g, hh):
        return x_copy(zb, hf, g, hh, xbuf.at[hf, window(g)[0], hh, 1], xsr.at[hf, g, hh, 1], xdev[1 - hh])

    def x_first(zb, hf, g, hh):
        return x_copy(zb, hf, g, hh, hbuf.at[hf, window(g)[0], hh], hsr.at[hf, g, hh], xdev[hh])

    def x_second(zb, hf, g, hh):
        return x_copy(zb, hf, g, hh, xbuf.at[hf, window(g)[0], hh, 0], xsr.at[hf, g, hh, 0], xdev[hh])

    def merge(zb, hf, g):
        h, low, width = window(g)
        lanes = pl.ds(low, width)

        @pl.when(lax.rem(zb, 2) == c)
        def _():
            core_copy(zb, hf, g).wait_recv()
            ks[zb, hf, h, :, :, lanes] = ks[zb, hf, h, :, :, lanes] + rbuf[lax.div(zb, 2), hf, h, :, :, lanes]
            for hh in (0, 1):
                @pl.when(place(zb, hh) == 2)
                def _():
                    x_first(zb, hf, g, hh).start()

                @pl.when(place(zb, hh) == 3)
                def _():
                    x_direct(zb, hf, g, hh).start()

    def pass_on(zb, hf, g):
        h, low, width = window(g)
        lanes = pl.ds(low, width)
        for hh in (0, 1):
            @pl.when(jnp.logical_and(lax.rem(zb, 2) == c, place(zb, hh) == 1))
            def _():
                x_first(zb, hf, g, hh).wait_recv()
                rows = pl.ds(2 * hh, 2)
                ks[zb, hf, h, rows, :, lanes] = ks[zb, hf, h, rows, :, lanes] + hbuf[hf, h, hh, :, :, lanes]
                x_second(zb, hf, g, hh).start()

    for hf in range(H):
        mate_m(hf).start()
        beside_a(hf).start()
        if hf == 0:
            ring(0, 0, 1, 0, True).start()
            ring(1, 0, 1, 0, True).start()
    mate_b(0).start()
    mate_b(1).start()
    beside_a(0).wait_recv()
    ring(0, 0, 1, 1, True).start()
    ring(1, 0, 1, 1, True).start()
    mate_m(0).wait_recv()
    ring(0, 0, 1, 2, True).start()
    ring(1, 0, 1, 2, True).start()
    beside_b(z, 0, True).start()
    loads[2].wait()

    def blocks(t):
        return (z,) if t == 0 else (far,) if t == 4 else (mod(z - t, 8), mod(z + t, 8))

    far = mod(z + 4, 8)

    def arrived(hf, t):
        for zb in blocks(t):
            beside_b(zb, hf, False).wait_recv()

    def many(first, count, hf, g, *works):
        for work in works:
            @pl.loop(0, count)
            def _(n):
                work(mod(z + first + n, 8), hf, g)

    def each(hf, t, g, *works):
        for work in works:
            for zb in blocks(t):
                work(zb, hf, g)

    def do(f, *rest):
        return lambda: f(*rest)

    fill = {}

    def put(hf, t, p, f, *rest):
        fill.setdefault((hf, t, p), []).append(do(f, *rest))

    for hf in range(H):
        for t in (0, 1, 2, 3):
            put(hf, t + 1, 1, arrived, hf, t)
            put(hf, t + 1, 1, each, hf, t, 0, unit)
            put(hf, t + 1, 2, each, hf, t, 0, merge)
            if t < 3:
                put(hf, t + 2, 0, each, hf, t, 0, pass_on)
    put(1, 1, 0, each, 0, 3, 0, pass_on)
    put(1, 1, 0, arrived, 0, 4)
    put(1, 1, 0, each, 0, 4, 0, unit)
    put(1, 1, 1, each, 0, 4, 0, merge)
    put(1, 1, 1, mate_b(0).wait_recv)
    put(1, 1, 2, many, -1, 3, 0, 1, unit, merge)
    put(1, 2, 0, each, 0, 4, 0, pass_on)
    put(1, 2, 1, many, -1, 3, 0, 1, pass_on)
    put(1, 2, 1, many, 2, 5, 0, 1, unit)
    put(1, 2, 2, many, 2, 5, 0, 1, merge)
    put(1, 3, 0, many, 2, 5, 0, 1, pass_on)
    put(1, 3, 1, many, -1, 3, 1, 1, unit)
    put(1, 3, 2, many, -1, 3, 1, 1, merge)
    put(1, 4, 0, many, -1, 3, 1, 1, pass_on)

    for hf in range(H):
        for t in (1, 2, 3, 4):
            for p in range(3):
                for way in (0, 1):
                    if (way, t, p) in ring_steps:
                        ring(way, hf, t, p, False).wait_recv()
                    if (way, t + 1, p) in ring_steps:
                        ring(way, hf, t + 1, p, True).start()
                    if p == 2 and t < 4:
                        beside_b(blocks(t)[way], hf, True).start()
                if p == 2 and t == 4:
                    beside_b(far, hf, True).start()
                if t == 3 and hf + 1 < H:
                    if p == 1:
                        beside_a(hf + 1).wait_recv()
                    if p == 2:
                        mate_m(hf + 1).wait_recv()
                        beside_b(z, hf + 1, True).start()
                    for way in (0, 1):
                        ring(way, hf + 1, 1, p, True).start()
                for work in fill.get((hf, t, p), ()):
                    work()
                if p == 1 and t == 1 and hf == 0:
                    m2_stage(0)
                if p == 2:
                    m2_stage(5 * hf + t)
                    if t == 4 and hf + 1 < H:
                        m2_stage(5 * (hf + 1))

    def oq_part(hf, s):
        return oq.at[hf, :, pl.ds(pl.multiple_of(512 * s, 512), 512)]

    def oq_copy(hf, h, sent):
        s = ((y, yp) if sent else (y1, y1p))[h]
        return remote(oq_part(hf, s), oq_part(hf, s), oqs.at[hf, h], oqr.at[hf, h], beside)

    def off_here(hf):
        return pltpu.make_async_copy(ks.at[i, hf, 0], off_ref.at[a, :, hf], offs.at[hf, 0])

    def off_there(hf):
        return remote(ks.at[i, hf, 1], off_ref.at[a, :, hf], offs.at[hf, 1], offr.at[hf], mate)

    def finish(hf, h):
        for hh in (0, 1):
            for g in (0,) if h == 0 else (1, 2):
                x_direct(i, hf, g, hh).wait_recv()
                x_second(i, hf, g, hh).wait_recv()
            rows = pl.ds(2 * hh, 2)
            ks[i, hf, h, rows] = -((ks[i, hf, h, rows] + xbuf[hf, h, hh, 0]) + xbuf[hf, h, hh, 1])
        s = (y, yp)[h]
        oq[hf, :, pl.ds(pl.multiple_of(512 * s, 512), 512)] = ks[i, hf, h].reshape(WR, 512).astype(BF16)
        oq_copy(hf, h, True).start()
        (off_here, off_there)[h](hf).start()

    def second(hf):
        for h in (0, 1):
            oq_copy(hf, h, False).wait_recv()

        @pl.loop(0, 8)
        def _(zb):
            pt[hf, zb] = lax.dot_general(m2[zb], oq[hf], (((1,), (1,)), ((), ())), preferred_element_type=F32)

    def z_copy(hf, way, k, kind):
        zb = mod(z + (-1 if way else 1) * (5 - k), 8)
        return remote(
            pt.at[hf, zb, pl.ds(64 * kind, 64)], zbuf.at[hf, way, k - 1, kind],
            zss.at[hf, way, k, kind], zsr.at[hf, way, k, kind], zdev[way],
        )

    def z_has(way, k, kind):
        return k > 1 or kind == way

    def z_sum(hf, k):
        for kind in (0, 1):
            for way in (0, 1):
                if k > 1 and z_has(way, k - 1, kind):
                    z_copy(hf, way, k - 1, kind).wait_recv()
                    zb = mod(z + (-1 if way else 1) * (5 - k), 8)
                    rows = pl.ds(64 * kind, 64)
                    pt[hf, zb, rows] = pt[hf, zb, rows] + zbuf[hf, way, k - 2, kind]
                if k < 5 and z_has(way, k, kind):
                    z_copy(hf, way, k, kind).start()

    def dfin_copy(hf):
        return remote(pt.at[hf, z, pl.ds(64, 64)], dfin.at[hf], dfs.at[hf], dfr.at[hf], mate)

    def drain():
        mate_b(0).wait_send()
        mate_b(1).wait_send()
        for hf in range(H):
            mate_m(hf).wait_send()
            beside_a(hf).wait_send()
            for way, t, p in ring_steps:
                ring(way, hf, t, p, True).wait_send()

        @pl.loop(0, 8)
        def _(zb):
            for hf in range(H):
                beside_b(zb, hf, True).wait_send()
                for g in range(3):
                    @pl.when(lax.rem(zb, 2) != c)
                    def _():
                        core_copy(zb, hf, g).wait_send()

                    @pl.when(jnp.logical_and(lax.rem(zb, 2) == c, lax.div(zb, 2) != x))
                    def _():
                        for hh in (0, 1):
                            x_first(zb, hf, g, hh).wait_send()

                for kind in (0, 1):
                    @pl.when(col)
                    def _():
                        m2_across(zb, hf, kind, False).wait_send()

                        @pl.when(jnp.logical_or(e == 0, hops(kind) < 3))
                        def _():
                            m2_along(zb, hf, kind, False).wait_send()

    finish(0, 0)
    mate_b(1).wait_recv()
    many(0, 8, 0, 2, unit, merge)
    each(1, 3, 0, pass_on)
    arrived(1, 4)
    each(1, 4, 0, unit)
    many(2, 5, 1, 1, unit)
    each(1, 4, 0, merge)
    many(0, 8, 0, 2, pass_on)
    many(2, 5, 1, 1, merge)
    m2_stage(5 * H)
    many(0, 8, 1, 2, unit)
    finish(0, 1)
    many(0, 8, 1, 2, merge)
    each(1, 4, 0, pass_on)
    many(2, 5, 1, 1, pass_on)
    m2_stage(5 * H + 1)
    many(0, 8, 1, 2, pass_on)
    m2_stage(5 * H + 2)
    finish(1, 0)

    @pl.loop(0, 16)
    def _(q):
        zb, kind = lax.div(q, 2), lax.rem(q, 2)
        for hf in range(H):
            @pl.when(source)
            def _():
                m2_here(zb, hf, kind).wait()

            @pl.when(jnp.logical_not(col))
            def _():
                m2_across(zb, hf, kind, False).wait_recv()

    second(0)
    z_sum(0, 1)
    finish(1, 1)
    z_sum(0, 2)
    z_sum(0, 3)
    second(1)
    z_sum(1, 1)
    z_sum(0, 4)
    z_sum(1, 2)
    z_sum(0, 5)
    dfin_copy(0).start()
    z_sum(1, 3)
    drain()
    z_sum(1, 4)
    z_sum(1, 5)
    dfin_copy(1).start()

    def lanes_in_order(parts):
        return jnp.concatenate([parts[hf][:, SR * s : SR * (s + 1)] for s in range(4) for hf in range(H)], axis=1)

    loads[3].wait()
    diag_ref[a] = dinv_ref[a] - lanes_in_order([pt[hf, z, pl.ds(0, 64)] for hf in range(H)])
    for hf in range(H):
        dfin_copy(hf).wait_recv()
    diag_ref[1 - a] = dinv_ref[1 - a] - lanes_in_order([dfin[hf] for hf in range(H)])

    for hf in range(H):
        dfin_copy(hf).wait_send()
        off_here(hf).wait()
        off_there(hf).wait()
        for h in (0, 1):
            oq_copy(hf, h, True).wait_send()
        for k in (1, 2, 3, 4):
            for kind in (0, 1):
                for way in (0, 1):
                    if z_has(way, k, kind):
                        z_copy(hf, way, k, kind).wait_send()


def shards(anc_mask, factor, inverse_block, diag_inverse):
    vmem = pl.BlockSpec(memory_space=pltpu.VMEM)
    hbm = pl.BlockSpec(memory_space=pl.ANY)
    dma = pltpu.SemaphoreType.DMA
    off, diag = pl.pallas_call(
        kernel,
        out_shape=(jax.ShapeDtypeStruct((2, 4, H, SR, 512), F32), jax.ShapeDtypeStruct((2, 64, 256), F32)),
        in_specs=[hbm, hbm, hbm, hbm],
        out_specs=(hbm, vmem),
        scratch_shapes=[
            pltpu.SMEM((2, 16), jnp.int32),
            pltpu.VMEM((2, 64, 2048), BF16),
            pltpu.VMEM((2, 64, 256), F32),
            pltpu.VMEM((8, H, 4, SR, 2048), BF16),
            pltpu.VMEM((2048, 512), BF16),
            pltpu.VMEM((2048, 512), BF16),
            pltpu.VMEM((H, SR, 2048), BF16),
            pltpu.VMEM((8, H, 2, 4, SR, 512), F32),
            pltpu.VMEM((4, H, 2, 4, SR, 512), F32),
            pltpu.VMEM((H, 2, 2, 2, 2, SR, 512), F32),
            pltpu.VMEM((H, 2, 2, 2, SR, 512), F32),
            pltpu.VMEM((8, 128, 2048), BF16),
            pltpu.VMEM((H, WR, 2048), BF16),
            pltpu.VMEM((H, 8, 128, WR), F32),
            pltpu.VMEM((H, 2, 4, 2, 64, WR), F32),
            pltpu.VMEM((H, 64, WR), F32),
            dma((H, 2, 5, 3)), dma((H, 2, 5, 3)),
            dma((H,)), dma((H,)),
            dma((H, 8)), dma((H, 8)),
            dma((H,)), dma((H,)),
            dma((2,)), dma((2,)),
            dma((H, 3, 8)), dma((H, 3, 8)),
            dma((H, 3, 2, 8)), dma((H, 3, 2, 2)), dma((H, 3, 2)),
            dma((H, 2, 8)), dma((H, 2, 8)), dma((H, 2, 8)), dma((H, 2, 8)), dma((H, 2, 8)),
            dma((H, 2)), dma((H, 2)),
            dma((H, 2)), dma((H,)),
            dma((H, 2, 5, 2)), dma((H, 2, 5, 2)),
            dma((H,)), dma((H,)),
            dma((4,)),
        ],
        compiler_params=pltpu.CompilerParams(
            collective_id=0, has_side_effects=True, vmem_limit_bytes=62 * 2**20
        ),
        cost_estimate=pl.CostEstimate(flops=9663676416, bytes_accessed=2**23, transcendentals=0),
        name="selected_inverse",
    )(anc_mask, factor.transpose(0, 2, 1), inverse_block, diag_inverse.transpose(0, 2, 1))
    return off.reshape(2, 256, 512), diag.transpose(0, 2, 1)


def solution(mesh):
    placed = (P(None, "prow"), P(None, "prow", "pcol"), P("prow", "pcol"), P(None, "prow", "pcol"))
    return jax.shard_map(
        shards,
        mesh=mesh,
        in_specs=placed,
        out_specs=(P(None, "prow", "pcol"), P(None, "prow", "pcol")),
        check_vma=False,
    )
```

time: 537 us -> 149 us (0.28)
  waiting for transfers between devices: 491 us -> 0 us
  Pallas kernels: 0 us -> 145 us
  matrix products: 20 us -> 0 us
  between operations: 13.8 us -> 0.65 us
  other arithmetic: 10.5 us -> 0 us
    reduce_scatter x2 -> x0, waiting for transfers between devices: 268 us -> none  [the longest x1 223 us: shards(): lax.psum_scatter(partial_diag, 'pcol', scatter_dimension=2, tiled=True)]
    pallas_call x0 -> x1, Pallas kernels: none -> 145 us  [shards(): pl.pallas_call(kernel, out_shape=(jax.ShapeDtypeStruct((2, 4, H, SR, 512)...]
    all_gather x1 -> x0, waiting for transfers between devices: 145 us -> none  [shards(): gathered = lax.all_gather(masked, 'pcol', axis=2, tiled=True)]
    psum x1 -> x0, waiting for transfers between devices: 77.6 us -> none  [spread(): return lax.psum(kept, axis)]
    dot_general x2 -> x0, matrix products: 20 us -> none  [the longest x1 14.5 us: shards(): jnp.einsum('src,rq->csq', gathered, inverse_block, preferred_element_type...]
  transfers between devices with their start and end apart: 4 -> 0, of which waited for: 4 -> 0; matrix products, arithmetic and copies ran while one was open for 1% -> 0% of each run, Pallas kernels for 0% -> 0%
where the time goes in v2:
time: 149 us; the launch traced here: 148 us
  Pallas kernels  145 us (97%)
  local copies, waits for them, and re-layouts  2.96 us (2%)
    pallas_call x1, Pallas kernels, shards(): pl.pallas_call(kernel, out_shape=(jax.ShapeDtypeStruct((2, 4, H, SR, 512)...  145 us

profile of v2, /device:TPU:6, one launch (start us, length us, event | category | flops | bytes accessed | tf_op | source)
XLA Modules:
  0.0 148.4 jit_solution(3688190291152377577)
XLA Ops:
  0.6 144.8 %selected_inverse.1 = (f32[2,4,2,32,512]{4,3,2,1,0:T(8,128)}, f32[2,64,256]{2,1,0:T(8,128)}) custom-call(s32[2,16]{1,0:T(2,128)} %mask_hbm.1, bf16[2,64,2048]{2,1,0:T(8,128)(2,1)} %bitcast.6, bf16[2048,512]{1,0:T(8,128)(2,1)} %b_ref.1, f32[2,64,256]{2,1,0:T(8,128)} %bitcast.7), custom_call_target="tpu_custom_call" | custom-call | flops 9663676416 | bytes 8388608 | tf_op jit(solution)/shard_map/selected_inverse/pallas_call | solution.py:492
  145.5 0.0 copy-start
  145.5 2.3 %copy.8 = f32[2,256,512]{2,1,0:T(8,128)} copy(f32[2,256,512]{2,1,0:T(8,128)} %bitcast.4) | data formatting | bytes 2097152
  147.8 0.0 copy-done
  147.8 0.7 copy.9
Async XLA Ops:
  145.5 2.3 %copy-start = (f32[2,64,256]{2,1,0:T(8,128)S(1)}, f32[2,64,256]{2,1,0:T(8,128)}, u32[]{:S(2)}) copy-start(f32[2,64,256]{2,1,0:T(8,128)} %get-tuple-element.5) | copy-start | bytes 393220

commit v3 on v2

--- a/solution.py
+++ b/solution.py
@@ -8,7 +8,8 @@
 MESH = pl.DeviceIdType.MESH
 F32 = jnp.float32
 BF16 = jnp.bfloat16
-H = 2
+H = 1
+LAG = 2
 SR = 64 // H
 WR = 256 // H
 
@@ -37,7 +38,7 @@
     y1 = y + 1 - 2 * lax.rem(y, 2)
     yp = 3 - y
     y1p = 3 - y1
-    slots = (y, y1, yp)
+    slots = (y, yp, y1)
 
     def dev(x_, c_, z_, y_):
         return (2 * x_ + c_, 4 * z_ + y_)
@@ -55,7 +56,8 @@
     for load in loads:
         load.start()
     barrier = pltpu.get_barrier_semaphore()
-    greeted = [mate, beside, zdev[0], zdev[1], xdev[0], xdev[1], sib]
+    across = (dev(x, c, mod(z + 1, 8), yp), dev(x, c, mod(z - 1, 8), yp))
+    greeted = [mate, beside, zdev[0], zdev[1], xdev[0], xdev[1], sib, across[0], across[1]]
     for device in greeted:
         pl.semaphore_signal(barrier, inc=1, device_id=device, device_id_type=MESH)
     loads[0].wait()
@@ -77,19 +79,20 @@
         sign = 1 if way else -1
         zb = mod(z + sign * (t - 1 if sent else t), 8)
         part = mf.at[zb, hf, slots[p]]
-        if t == 4 and p == 2:
-            part = mf.at[zb, hf, slots[2], pl.ds(SR // 2 * way, SR // 2)]
+        if t == 4 and p == 1:
+            part = mf.at[zb, hf, slots[1], pl.ds(SR // 2 * way, SR // 2)]
         return remote(part, part, mzs.at[hf, way, t, p], mzr.at[hf, way, t, p], zdev[way])
 
     near_steps = [(way, t, p) for t in (1, 2, 3) for p in range(3) for way in (0, 1)]
-    far_steps = [(0, 4, 0), (1, 4, 1), (0, 4, 2), (1, 4, 2)]
+    far_steps = [(0, 4, 0), (0, 4, 1), (1, 4, 1), (1, 4, 2)]
     ring_steps = near_steps + far_steps
 
     def mate_m(hf):
         return remote(stage.at[hf], mf.at[z, hf, y], mms.at[hf], mmr.at[hf], mate)
 
     def mate_b(n):
-        lanes = pl.ds(256 * n, 256)
+        _, low, width = window(n + 1)
+        lanes = pl.ds(low, width)
         return remote(b_ref.at[:, lanes], b2.at[:, lanes], pts.at[n], ptr.at[n], mate)
 
     def beside_a(hf):
@@ -127,38 +130,39 @@
     def hops(kind):
         return e + kind * (4 - 2 * e)
 
-    def m2_stage(tau):
+    def m2_stage(sigma):
         @pl.loop(0, 4)
         def _(q):
             kind, way = lax.div(q, 2), lax.rem(q, 2)
-            if tau < 5 * H:
-                fits = jnp.logical_and(tau % 5 >= way, tau % 5 <= 4 - way)
+            if sigma % 3 == 2 and sigma <= 14:
+                step = sigma // 3
+                fits = jnp.logical_and(step >= way, step <= 4 - way)
 
                 @pl.when(jnp.logical_and(source, fits))
                 def _():
-                    zb = mod(z + (2 * way - 1) * (tau % 5), 8)
-                    m2_along(zb, tau // 5, kind, True).start()
-                    m2_across(zb, tau // 5, kind, True).start()
-                    m2_here(zb, tau // 5, kind).start()
-
-            n = tau - hops(kind)
-            t = lax.rem(n + 5, 5)
-            due = jnp.logical_and(jnp.logical_and(n >= 0, n < 5 * H), jnp.logical_and(t >= way, t <= 4 - way))
+                    zb = mod(z + (2 * way - 1) * step, 8)
+                    m2_along(zb, 0, kind, True).start()
+                    m2_across(zb, 0, kind, True).start()
+                    m2_here(zb, 0, kind).start()
+
+            n = sigma - 2 - LAG * hops(kind)
+            t = lax.div(n, 3)
+            whole = jnp.logical_and(n >= 0, lax.rem(n, 3) == 0)
+            due = jnp.logical_and(whole, jnp.logical_and(t >= way, t <= 4 - way))
 
             @pl.when(jnp.logical_and(relay, due))
             def _():
-                hf = lax.div(n, 5)
                 zb = mod(z + (2 * way - 1) * t, 8)
-                m2_along(zb, hf, kind, False).wait_recv()
+                m2_along(zb, 0, kind, False).wait_recv()
 
                 @pl.when(hops(kind) < 3)
                 def _():
-                    m2_along(zb, hf, kind, False).start()
-
-                m2_across(zb, hf, kind, False).start()
+                    m2_along(zb, 0, kind, False).start()
+
+                m2_across(zb, 0, kind, False).start()
 
     def window(g):
-        return (0, 0, 512) if g == 0 else (1, 256 * (g - 1), 256)
+        return ((0, 0, 512), (1, 0, 256), (1, 256, 128), (1, 384, 128))[g]
 
     def tile(ref, g, index, rows=pl.ds(0, 4)):
         h, low, width = window(g)
@@ -173,9 +177,12 @@
         h, low, width = window(g)
         left = mf[zb, hf].reshape(WR, 2048)
         right = (b1, b2)[h]
-        for at in range(low, low + width, 256):
-            lanes = pl.ds(at, 256)
-            ks[zb, hf, h, :, :, lanes] = jnp.dot(left, right[:, lanes], preferred_element_type=F32).reshape(4, SR, 256)
+        step = min(width, 256)
+
+        @pl.loop(0, width // step)
+        def _(n):
+            lanes = pl.ds(pl.multiple_of(low + step * n, step), step)
+            ks[zb, hf, h, :, :, lanes] = jnp.dot(left, right[:, lanes], preferred_element_type=F32).reshape(4, SR, step)
 
         @pl.when(lax.rem(zb, 2) != c)
         def _():
@@ -234,15 +241,15 @@
         if hf == 0:
             ring(0, 0, 1, 0, True).start()
             ring(1, 0, 1, 0, True).start()
-    mate_b(0).start()
-    mate_b(1).start()
-    beside_a(0).wait_recv()
+    for n in range(3):
+        mate_b(n).start()
+    mate_m(0).wait_recv()
     ring(0, 0, 1, 1, True).start()
     ring(1, 0, 1, 1, True).start()
-    mate_m(0).wait_recv()
+    beside_b(z, 0, True).start()
+    beside_a(0).wait_recv()
     ring(0, 0, 1, 2, True).start()
     ring(1, 0, 1, 2, True).start()
-    beside_b(z, 0, True).start()
     loads[2].wait()
 
     def blocks(t):
@@ -250,20 +257,17 @@
 
     far = mod(z + 4, 8)
 
-    def arrived(hf, t):
-        for zb in blocks(t):
-            beside_b(zb, hf, False).wait_recv()
-
-    def many(first, count, hf, g, *works):
-        for work in works:
-            @pl.loop(0, count)
-            def _(n):
-                work(mod(z + first + n, 8), hf, g)
-
-    def each(hf, t, g, *works):
-        for work in works:
-            for zb in blocks(t):
-                work(zb, hf, g)
+    def one(zb, *works):
+        for work, *rest in works:
+            work(zb, 0, *rest)
+
+    def arrive(zb, hf):
+        beside_b(zb, hf, False).wait_recv()
+
+    def many(first, count, hf, g, work):
+        @pl.loop(0, count)
+        def _(n):
+            work(mod(z + first + n, 8), hf, g)
 
     def do(f, *rest):
         return lambda: f(*rest)
@@ -273,28 +277,31 @@
     def put(hf, t, p, f, *rest):
         fill.setdefault((hf, t, p), []).append(do(f, *rest))
 
-    for hf in range(H):
-        for t in (0, 1, 2, 3):
-            put(hf, t + 1, 1, arrived, hf, t)
-            put(hf, t + 1, 1, each, hf, t, 0, unit)
-            put(hf, t + 1, 2, each, hf, t, 0, merge)
-            if t < 3:
-                put(hf, t + 2, 0, each, hf, t, 0, pass_on)
-    put(1, 1, 0, each, 0, 3, 0, pass_on)
-    put(1, 1, 0, arrived, 0, 4)
-    put(1, 1, 0, each, 0, 4, 0, unit)
-    put(1, 1, 1, each, 0, 4, 0, merge)
-    put(1, 1, 1, mate_b(0).wait_recv)
-    put(1, 1, 2, many, -1, 3, 0, 1, unit, merge)
-    put(1, 2, 0, each, 0, 4, 0, pass_on)
-    put(1, 2, 1, many, -1, 3, 0, 1, pass_on)
-    put(1, 2, 1, many, 2, 5, 0, 1, unit)
-    put(1, 2, 2, many, 2, 5, 0, 1, merge)
-    put(1, 3, 0, many, 2, 5, 0, 1, pass_on)
-    put(1, 3, 1, many, -1, 3, 1, 1, unit)
-    put(1, 3, 2, many, -1, 3, 1, 1, merge)
-    put(1, 4, 0, many, -1, 3, 1, 1, pass_on)
-
+    put(0, 1, 0, one, z, (arrive,), (unit, 0))
+    put(0, 1, 1, one, z, (merge, 0))
+    put(0, 1, 2, one, z, (pass_on, 0))
+    for t in (1, 2, 3):
+        low, high = blocks(t)
+        extra = ((), (1,), (1, 2))[t - 1]
+        put(0, t + 1, 0, one, low, (arrive,), (unit, 0), *[(unit, g) for g in extra])
+        put(0, t + 1, 1, one, low, (merge, 0), *[(merge, g) for g in extra])
+        put(0, t + 1, 1, one, high, (arrive,), (unit, 0), *[(unit, g) for g in extra])
+        put(0, t + 1, 2, one, high, (merge, 0), *[(merge, g) for g in extra])
+        put(0, t + 1, 2, one, low, (pass_on, 0), *[(pass_on, g) for g in extra])
+        if t < 3:
+            put(0, t + 2, 0, one, high, (pass_on, 0), *[(pass_on, g) for g in extra])
+    put(0, 2, 2, mate_b(0).wait_recv)
+    put(0, 2, 2, many, -1, 3, 0, 1, unit)
+    put(0, 3, 0, many, -1, 3, 0, 1, merge)
+    put(0, 3, 2, many, -1, 3, 0, 1, pass_on)
+    put(0, 3, 2, mate_b(1).wait_recv)
+    put(0, 3, 2, many, -2, 5, 0, 2, unit)
+    put(0, 4, 0, many, -2, 5, 0, 2, merge)
+    put(0, 4, 2, many, -2, 5, 0, 2, pass_on)
+    put(0, 4, 2, mate_b(2).wait_recv)
+    put(0, 4, 2, many, -3, 7, 0, 3, unit)
+
+    m2_stage(2)
     for hf in range(H):
         for t in (1, 2, 3, 4):
             for p in range(3):
@@ -303,9 +310,9 @@
                         ring(way, hf, t, p, False).wait_recv()
                     if (way, t + 1, p) in ring_steps:
                         ring(way, hf, t + 1, p, True).start()
-                    if p == 2 and t < 4:
+                    if p == 1 and t < 4:
                         beside_b(blocks(t)[way], hf, True).start()
-                if p == 2 and t == 4:
+                if p == 1 and t == 4:
                     beside_b(far, hf, True).start()
                 if t == 3 and hf + 1 < H:
                     if p == 1:
@@ -317,15 +324,10 @@
                         ring(way, hf + 1, 1, p, True).start()
                 for work in fill.get((hf, t, p), ()):
                     work()
-                if p == 1 and t == 1 and hf == 0:
-                    m2_stage(0)
-                if p == 2:
-                    m2_stage(5 * hf + t)
-                    if t == 4 and hf + 1 < H:
-                        m2_stage(5 * (hf + 1))
+                m2_stage(3 * t + p)
 
     def oq_part(hf, s):
-        return oq.at[hf, :, pl.ds(pl.multiple_of(512 * s, 512), 512)]
+        return oq.at[hf, pl.ds(pl.multiple_of(512 * s, 512), 512)]
 
     def oq_copy(hf, h, sent):
         s = ((y, yp) if sent else (y1, y1p))[h]
@@ -339,38 +341,51 @@
 
     def finish(hf, h):
         for hh in (0, 1):
-            for g in (0,) if h == 0 else (1, 2):
+            for g in (0,) if h == 0 else (1, 2, 3):
                 x_direct(i, hf, g, hh).wait_recv()
                 x_second(i, hf, g, hh).wait_recv()
             rows = pl.ds(2 * hh, 2)
             ks[i, hf, h, rows] = -((ks[i, hf, h, rows] + xbuf[hf, h, hh, 0]) + xbuf[hf, h, hh, 1])
         s = (y, yp)[h]
-        oq[hf, :, pl.ds(pl.multiple_of(512 * s, 512), 512)] = ks[i, hf, h].reshape(WR, 512).astype(BF16)
+        oq[hf, pl.ds(pl.multiple_of(512 * s, 512), 512)] = ks[i, hf, h].reshape(WR, 512).T.astype(BF16)
         oq_copy(hf, h, True).start()
         (off_here, off_there)[h](hf).start()
 
-    def second(hf):
+    def swapped(hf):
         for h in (0, 1):
             oq_copy(hf, h, False).wait_recv()
 
-        @pl.loop(0, 8)
-        def _(zb):
-            pt[hf, zb] = lax.dot_general(m2[zb], oq[hf], (((1,), (1,)), ((), ())), preferred_element_type=F32)
+    def second(hf, zb):
+        pt[hf, zb] = jnp.dot(m2[zb], oq[hf], preferred_element_type=F32)
 
     def z_copy(hf, way, k, kind):
         zb = mod(z + (-1 if way else 1) * (5 - k), 8)
+        part = pt.at[hf, zb, pl.ds(64 * kind, 64)]
+        if k == 4 and kind == 1:
+            return remote(part, dfin.at[hf, way], dfs.at[hf, way], dfr.at[hf, way], across[way])
         return remote(
-            pt.at[hf, zb, pl.ds(64 * kind, 64)], zbuf.at[hf, way, k - 1, kind],
-            zss.at[hf, way, k, kind], zsr.at[hf, way, k, kind], zdev[way],
+            part, zbuf.at[hf, way, k - 1, kind], zss.at[hf, way, k, kind], zsr.at[hf, way, k, kind], zdev[way]
         )
+
+    def dfin_copy(hf):
+        return remote(pt.at[hf, z, pl.ds(64, 64)], dfin.at[hf, 2], dfs.at[hf, 2], dfr.at[hf, 2], mate)
 
     def z_has(way, k, kind):
         return k > 1 or kind == way
 
     def z_sum(hf, k):
+        if k == 1:
+            second(hf, far)
+        if 1 < k < 5:
+            @pl.loop(0, 2)
+            def _(way):
+                second(hf, mod(z + (1 - 2 * way) * (5 - k), 8))
+        if k == 3:
+            second(hf, z)
+            dfin_copy(hf).start()
         for kind in (0, 1):
             for way in (0, 1):
-                if k > 1 and z_has(way, k - 1, kind):
+                if k > 1 and z_has(way, k - 1, kind) and not (k == 5 and kind == 1):
                     z_copy(hf, way, k - 1, kind).wait_recv()
                     zb = mod(z + (-1 if way else 1) * (5 - k), 8)
                     rows = pl.ds(64 * kind, 64)
@@ -378,12 +393,9 @@
                 if k < 5 and z_has(way, k, kind):
                     z_copy(hf, way, k, kind).start()
 
-    def dfin_copy(hf):
-        return remote(pt.at[hf, z, pl.ds(64, 64)], dfin.at[hf], dfs.at[hf], dfr.at[hf], mate)
-
     def drain():
-        mate_b(0).wait_send()
-        mate_b(1).wait_send()
+        for n in range(3):
+            mate_b(n).wait_send()
         for hf in range(H):
             mate_m(hf).wait_send()
             beside_a(hf).wait_send()
@@ -394,7 +406,7 @@
         def _(zb):
             for hf in range(H):
                 beside_b(zb, hf, True).wait_send()
-                for g in range(3):
+                for g in range(4):
                     @pl.when(lax.rem(zb, 2) != c)
                     def _():
                         core_copy(zb, hf, g).wait_send()
@@ -413,26 +425,25 @@
                         def _():
                             m2_along(zb, hf, kind, False).wait_send()
 
+    arrive(far, 0)
+    for g in range(4):
+        unit(far, 0, g)
+    m2_stage(15)
+    m2_stage(16)
+    many(-3, 7, 0, 3, merge)
+    for g in range(4):
+        merge(far, 0, g)
+    for g in (0, 1, 2):
+        pass_on(blocks(3)[1], 0, g)
+    many(-3, 7, 0, 3, pass_on)
+    m2_stage(17)
+    for g in range(4):
+        pass_on(far, 0, g)
     finish(0, 0)
-    mate_b(1).wait_recv()
-    many(0, 8, 0, 2, unit, merge)
-    each(1, 3, 0, pass_on)
-    arrived(1, 4)
-    each(1, 4, 0, unit)
-    many(2, 5, 1, 1, unit)
-    each(1, 4, 0, merge)
-    many(0, 8, 0, 2, pass_on)
-    many(2, 5, 1, 1, merge)
-    m2_stage(5 * H)
-    many(0, 8, 1, 2, unit)
+    m2_stage(18)
     finish(0, 1)
-    many(0, 8, 1, 2, merge)
-    each(1, 4, 0, pass_on)
-    many(2, 5, 1, 1, pass_on)
-    m2_stage(5 * H + 1)
-    many(0, 8, 1, 2, pass_on)
-    m2_stage(5 * H + 2)
-    finish(1, 0)
+    m2_stage(20)
+    drain()
 
     @pl.loop(0, 16)
     def _(q):
@@ -446,22 +457,9 @@
             def _():
                 m2_across(zb, hf, kind, False).wait_recv()
 
-    second(0)
-    z_sum(0, 1)
-    finish(1, 1)
-    z_sum(0, 2)
-    z_sum(0, 3)
-    second(1)
-    z_sum(1, 1)
-    z_sum(0, 4)
-    z_sum(1, 2)
-    z_sum(0, 5)
-    dfin_copy(0).start()
-    z_sum(1, 3)
-    drain()
-    z_sum(1, 4)
-    z_sum(1, 5)
-    dfin_copy(1).start()
+    swapped(0)
+    for k in (1, 2, 3, 4, 5):
+        z_sum(0, k)
 
     def lanes_in_order(parts):
         return jnp.concatenate([parts[hf][:, SR * s : SR * (s + 1)] for s in range(4) for hf in range(H)], axis=1)
@@ -469,8 +467,12 @@
     loads[3].wait()
     diag_ref[a] = dinv_ref[a] - lanes_in_order([pt[hf, z, pl.ds(0, 64)] for hf in range(H)])
     for hf in range(H):
+        z_copy(hf, 0, 4, 1).wait_recv()
+        z_copy(hf, 1, 4, 1).wait_recv()
         dfin_copy(hf).wait_recv()
-    diag_ref[1 - a] = dinv_ref[1 - a] - lanes_in_order([dfin[hf] for hf in range(H)])
+    diag_ref[1 - a] = dinv_ref[1 - a] - lanes_in_order(
+        [(dfin[hf, 0] + dfin[hf, 1]) + dfin[hf, 2] for hf in range(H)]
+    )
 
     for hf in range(H):
         dfin_copy(hf).wait_send()
@@ -507,26 +509,26 @@
             pltpu.VMEM((H, 2, 2, 2, 2, SR, 512), F32),
             pltpu.VMEM((H, 2, 2, 2, SR, 512), F32),
             pltpu.VMEM((8, 128, 2048), BF16),
-            pltpu.VMEM((H, WR, 2048), BF16),
+            pltpu.VMEM((H, 2048, WR), BF16),
             pltpu.VMEM((H, 8, 128, WR), F32),
             pltpu.VMEM((H, 2, 4, 2, 64, WR), F32),
-            pltpu.VMEM((H, 64, WR), F32),
+            pltpu.VMEM((H, 3, 64, WR), F32),
             dma((H, 2, 5, 3)), dma((H, 2, 5, 3)),
             dma((H,)), dma((H,)),
             dma((H, 8)), dma((H, 8)),
             dma((H,)), dma((H,)),
-            dma((2,)), dma((2,)),
-            dma((H, 3, 8)), dma((H, 3, 8)),
-            dma((H, 3, 2, 8)), dma((H, 3, 2, 2)), dma((H, 3, 2)),
+            dma((3,)), dma((3,)),
+            dma((H, 4, 8)), dma((H, 4, 8)),
+            dma((H, 4, 2, 8)), dma((H, 4, 2, 2)), dma((H, 4, 2)),
             dma((H, 2, 8)), dma((H, 2, 8)), dma((H, 2, 8)), dma((H, 2, 8)), dma((H, 2, 8)),
             dma((H, 2)), dma((H, 2)),
             dma((H, 2)), dma((H,)),
             dma((H, 2, 5, 2)), dma((H, 2, 5, 2)),
-            dma((H,)), dma((H,)),
+            dma((H, 3)), dma((H, 3)),
             dma((4,)),
         ],
         compiler_params=pltpu.CompilerParams(
-            collective_id=0, has_side_effects=True, vmem_limit_bytes=62 * 2**20
+            collective_id=0, has_side_effects=True, vmem_limit_bytes=58 * 2**20
         ),
         cost_estimate=pl.CostEstimate(flops=9663676416, bytes_accessed=2**23, transcendentals=0),
         name="selected_inverse",

time: 149 us -> 145 us (0.973)
  Pallas kernels: 145 us -> 140 us
    pallas_call x1, Pallas kernels: 145 us -> 140 us  [shards(): pl.pallas_call(kernel, out_shape=(jax.ShapeDtypeStruct((2, 4, H, SR, 512)...]
where the time goes in v3:
time: 145 us; the launch traced here: 144 us
  Pallas kernels  140 us (97%)
  local copies, waits for them, and re-layouts  2.96 us (2%)
    pallas_call x1, Pallas kernels, shards(): pl.pallas_call(kernel, out_shape=(jax.ShapeDtypeStruct((2, 4, H, SR, 512)...  140 us
    unnamed x4, local copies, waits for them, and re-layouts  2.96 us

profile of v3, /device:TPU:6, one launch (start us, length us, event | category | flops | bytes accessed | tf_op | source)
XLA Modules:
  0.0 144.0 jit_solution(10107839942703547736)
XLA Ops:
  0.6 140.4 %selected_inverse.1 = (f32[2,4,1,64,512]{4,3,2,1,0:T(8,128)}, f32[2,64,256]{2,1,0:T(8,128)}) custom-call(s32[2,16]{1,0:T(2,128)} %mask_hbm.1, bf16[2,64,2048]{2,1,0:T(8,128)(2,1)} %bitcast.6, bf16[2048,512]{1,0:T(8,128)(2,1)} %b_ref.1, f32[2,64,256]{2,1,0:T(8,128)} %bitcast.7), custom_call_target="tpu_custom_call" | custom-call | flops 9663676416 | bytes 8388608 | tf_op jit(solution)/shard_map/selected_inverse/pallas_call | solution.py:494
  141.0 0.0 copy-start
  141.0 2.3 %copy.8 = f32[2,256,512]{2,1,0:T(8,128)} copy(f32[2,256,512]{2,1,0:T(8,128)} %bitcast.4) | data formatting | bytes 2097152
  143.3 0.0 copy-done
  143.3 0.7 copy.9
Async XLA Ops:
  141.0 2.3 %copy-start = (f32[2,64,256]{2,1,0:T(8,128)S(1)}, f32[2,64,256]{2,1,0:T(8,128)}, u32[]{:S(2)}) copy-start(f32[2,64,256]{2,1,0:T(8,128)} %get-tuple-element.5) | copy-start | bytes 393220

commit v4 on v3

--- a/solution.py
+++ b/solution.py
@@ -280,24 +280,23 @@
     put(0, 1, 0, one, z, (arrive,), (unit, 0))
     put(0, 1, 1, one, z, (merge, 0))
     put(0, 1, 2, one, z, (pass_on, 0))
+    put(0, 2, 2, mate_b(0).wait_recv)
+    put(0, 2, 2, many, -1, 3, 0, 1, unit)
+    put(0, 3, 0, many, -1, 3, 0, 1, merge)
     for t in (1, 2, 3):
         low, high = blocks(t)
         extra = ((), (1,), (1, 2))[t - 1]
-        put(0, t + 1, 0, one, low, (arrive,), (unit, 0), *[(unit, g) for g in extra])
-        put(0, t + 1, 1, one, low, (merge, 0), *[(merge, g) for g in extra])
-        put(0, t + 1, 1, one, high, (arrive,), (unit, 0), *[(unit, g) for g in extra])
-        put(0, t + 1, 2, one, high, (merge, 0), *[(merge, g) for g in extra])
-        put(0, t + 1, 2, one, low, (pass_on, 0), *[(pass_on, g) for g in extra])
-        if t < 3:
-            put(0, t + 2, 0, one, high, (pass_on, 0), *[(pass_on, g) for g in extra])
-    put(0, 2, 2, mate_b(0).wait_recv)
-    put(0, 2, 2, many, -1, 3, 0, 1, unit)
-    put(0, 3, 0, many, -1, 3, 0, 1, merge)
-    put(0, 3, 2, many, -1, 3, 0, 1, pass_on)
-    put(0, 3, 2, mate_b(1).wait_recv)
-    put(0, 3, 2, many, -2, 5, 0, 2, unit)
-    put(0, 4, 0, many, -2, 5, 0, 2, merge)
-    put(0, 4, 2, many, -2, 5, 0, 2, pass_on)
+        put(0, t, 2, one, low, (arrive,), (unit, 0), *[(unit, g) for g in extra])
+        put(0, t + 1, 0, one, low, (merge, 0), *[(merge, g) for g in extra])
+        put(0, t + 1, 0, one, high, (arrive,), (unit, 0), *[(unit, g) for g in extra])
+        put(0, t + 1, 1, one, high, (merge, 0), *[(merge, g) for g in extra])
+        put(0, t + 1, 1, one, low, (pass_on, 0), *[(pass_on, g) for g in extra])
+        put(0, t + 1, 2, one, high, (pass_on, 0), *[(pass_on, g) for g in extra])
+    put(0, 3, 1, many, -1, 3, 0, 1, pass_on)
+    put(0, 3, 1, mate_b(1).wait_recv)
+    put(0, 3, 1, many, -2, 5, 0, 2, unit)
+    fill[(0, 3, 2)].insert(0, do(many, -2, 5, 0, 2, merge))
+    put(0, 4, 1, many, -2, 5, 0, 2, pass_on)
     put(0, 4, 2, mate_b(2).wait_recv)
     put(0, 4, 2, many, -3, 7, 0, 3, unit)
 
@@ -433,8 +432,6 @@
     many(-3, 7, 0, 3, merge)
     for g in range(4):
         merge(far, 0, g)
-    for g in (0, 1, 2):
-        pass_on(blocks(3)[1], 0, g)
     many(-3, 7, 0, 3, pass_on)
     m2_stage(17)
     for g in range(4):

time: 145 us -> 144 us (level)
  no operation moved by 1% of the time
where the time goes in v4:
time: 144 us
  Pallas kernels  140 us (97%)
  local copies, waits for them, and re-layouts  2.96 us (2%)
    pallas_call x1, Pallas kernels, shards(): pl.pallas_call(kernel, out_shape=(jax.ShapeDtypeStruct((2, 4, H, SR, 512)...  140 us
    unnamed x4, local copies, waits for them, and re-layouts  2.96 us

profile of v4, /device:TPU:6, one launch (start us, length us, event | category | flops | bytes accessed | tf_op | source)
XLA Modules:
  0.0 143.7 jit_solution(2453936269220095737)
XLA Ops:
  0.6 140.1 %selected_inverse.1 = (f32[2,4,1,64,512]{4,3,2,1,0:T(8,128)}, f32[2,64,256]{2,1,0:T(8,128)}) custom-call(s32[2,16]{1,0:T(2,128)} %mask_hbm.1, bf16[2,64,2048]{2,1,0:T(8,128)(2,1)} %bitcast.6, bf16[2048,512]{1,0:T(8,128)(2,1)} %b_ref.1, f32[2,64,256]{2,1,0:T(8,128)} %bitcast.7), custom_call_target="tpu_custom_call" | custom-call | flops 9663676416 | bytes 8388608 | tf_op jit(solution)/shard_map/selected_inverse/pallas_call | solution.py:491
  140.7 0.0 copy-start
  140.7 2.3 %copy.8 = f32[2,256,512]{2,1,0:T(8,128)} copy(f32[2,256,512]{2,1,0:T(8,128)} %bitcast.4) | data formatting | bytes 2097152
  143.0 0.0 copy-done
  143.0 0.7 copy.9
Async XLA Ops:
  140.7 2.3 %copy-start = (f32[2,64,256]{2,1,0:T(8,128)S(1)}, f32[2,64,256]{2,1,0:T(8,128)}, u32[]{:S(2)}) copy-start(f32[2,64,256]{2,1,0:T(8,128)} %get-tuple-element.5) | copy-start | bytes 393220
